TPU v7x, 32 devices: a whole 2x2x4 slice. The times are simulated.
32 devices in a mesh: pole: 2 (over x), prow: 8 (over z, y), pcol: 2 (over core).
Axes of the slice: x: 2, y: 2, z: 4, core: 2. Of those that a mesh axis runs over, the one named last changes fastest.
Arguments:
- ancestor_inverse: bfloat16 [8192, 4096], P(('pole', 'prow'), 'pcol'), parts along dimension 0, may hold values from -6 to 6
- l_panel: bfloat16 [8192, 1024], P(('pole', 'prow'), 'pcol'), parts along dimension 0, may hold values from -0.125 to 0.125
- diag_inverse: float32 [2048, 256], P(('pole', 'pcol')), parts along dimension 0, may hold values from -6 to 6
- pattern: int32 [4, 8], replicated, may hold values from 0 to 15, as said below
Outputs:
- column_blocks: float32 [8192, 1024], P(('pole', 'prow'), 'pcol'), parts along dimension 0
- diag_blocks: float32 [2048, 256], P(('pole', 'pcol')), parts along dimension 0
There are 2 independent parts, one for each index of `pole`. A program takes and returns all parts, laid end to end along the dimension named above; an argument that names none is the same for every part. Nothing has to cross between parts.
Inputs may be any that keep to these rules, and one draw needn't show every extreme that they name: `pattern`: each row lists 8 different ancestor supernodes in increasing order, and every row lists ancestor 16 - 1.
All inputs are finite; a program needn't handle non-finite values.
Results may differ from a plain program's by a relative error of at most 0.0003.
Values may be sent and summed in bfloat16 or wider, within the bound.
A program may use at most 128 MiB of HBM per device.

v0:
```python
import jax
import jax.numpy as jnp
from jax import lax
from jax.sharding import PartitionSpec as P

B = 256


def per_device(ancestor_inverse, l_panel, diag_inverse, pattern):
    row_index = lax.axis_index("prow")
    col_index = lax.axis_index("pcol")
    local_tiles = l_panel.shape[0] // B
    local_nodes = l_panel.shape[1] // B
    tile_ids = row_index * local_tiles + jnp.arange(local_tiles, dtype=jnp.int32)
    node_rows = lax.dynamic_slice_in_dim(pattern, col_index * local_nodes, local_nodes, 0)
    member = jnp.any(node_rows[None, :, :] == tile_ids[:, None, None], axis=2)
    panel_mask = member.astype(jnp.float32)[:, None, :, None]
    masked = (
        l_panel.reshape(local_tiles, B, local_nodes, B) * panel_mask.astype(jnp.bfloat16)
    ).reshape(l_panel.shape)
    swapped = lax.all_to_all(masked, "pcol", split_axis=0, concat_axis=1, tiled=True)
    partial_sum = jnp.dot(
        ancestor_inverse,
        lax.all_gather(swapped, "prow", axis=0, tiled=True),
        preferred_element_type=jnp.float32,
    )
    summed = lax.psum_scatter(partial_sum, "pcol", scatter_dimension=1, tiled=True)
    negated = -summed
    diag_terms = jnp.einsum(
        "rkb,rkc->kbc",
        masked.astype(jnp.float32).reshape(-1, local_nodes, B),
        negated.reshape(-1, local_nodes, B),
        precision=lax.Precision.HIGHEST,
    )
    totals = lax.psum(diag_terms, "prow")
    diag_blocks = diag_inverse - totals.reshape(local_nodes * B, B)
    column_blocks = (negated.reshape(local_tiles, B, local_nodes, B) * panel_mask).reshape(
        negated.shape
    )
    return (column_blocks, diag_blocks)


def solution(mesh):
    return jax.shard_map(
        per_device,
        mesh=mesh,
        in_specs=(
            P(("pole", "prow"), "pcol"),
            P(("pole", "prow"), "pcol"),
            P(("pole", "pcol"), None),
            P(),
        ),
        out_specs=(P(("pole", "prow"), "pcol"), P(("pole", "pcol"), None)),
        check_vma=False,
    )
```

profile of v0, /device:TPU:0, one launch (start us, length us, event | category | flops | bytes accessed | tf_op | source)
XLA Modules:
  0.0 193.3 jit_solution(15879236275212393171)
XLA Ops:
  7.2 0.0 copy-start
  7.2 0.0 all-gather.2.cloned.1.call-start
  7.2 0.8 constant_dynamic-slice_fusion
  8.1 0.2 compare_reduce_fusion
  8.3 0.3 mul.39
  8.6 0.1 copy.27
  8.7 1.2 mul.41
  9.9 4.2 %all_to_all.19 = bf16[2,256,512]{2,1,0:T(8,128)(2,1)S(1)} all-to-all(bf16[2,256,512]{2,1,0:T(8,128)(2,1)S(1)} %bitcast.30), channel_id=1, replica_groups=mesh['pole'=2,'prow'=8,'pcol'=2] {'pcol'}, dimensions={0} | all-to-all | bytes 1048576 | tf_op jit(solution)/shard_map/all_to_all | solution.py:21
  14.1 1.0 copy.19
  15.1 0.0 all-gather.2.cloned.1.call-update
  15.1 0.0 reduce-scatter.2.cloned.1.call-start
  15.1 77.8 %all-gather.2.cloned.1.call-done = bf16[2048,1024]{0,1:T(8,128)(2,1)} async-done(((bf16[256,1024]{0,1:T(8,128)(2,1)}), bf16[2048,1024]{0,1:T(8,128)(2,1)}) %all-gather.2.cloned.1.call-update) | async-done | bytes 4194320 | tf_op jit(solution)/shard_map/all_gather | solution.py:24
  93.0 0.0 copy-done
  93.0 5.9 %convolution_bitcast_fusion = f32[512,1024]{0,1:T(8,128)} fusion(bf16[2048,1024]{0,1:T(8,128)(2,1)} %all-gather.2.cloned.1.call-done, bf16[512,2048]{1,0:T(8,128)(2,1)S(1)} %copy-done), kind=kOutput, calls=%fused_computation | convolution fusion | flops 2147483648 | bytes 8388608 | tf_op jit(solution)/shard_map/dot_general | solution.py:22
  98.8 0.0 copy-start.1
  98.8 0.0 reduce-scatter.2.cloned.1.call-update
  98.9 0.0 all-reduce.2.cloned.1.call-start
  98.9 0.1 copy.21
  99.0 0.9 copy-done.1
  99.9 1.0 copy.26
  100.9 0.1 copy.20
  101.0 0.3 mul.42
  101.3 1.0 copy.28
  102.4 0.1 broadcast_bitcast_fusion
  102.4 4.4 %reduce-scatter.2.cloned.1.call-done = f32[512,512]{0,1:T(8,128)} async-done(((f32[512,1024]{0,1:T(8,128)}), f32[512,512]{0,1:T(8,128)}) %reduce-scatter.2.cloned.1.call-update) | async-done | bytes 1048592 | tf_op jit(solution)/shard_map/reduce_scatter | solution.py:27
  106.8 0.0 copy-start.2
  106.8 1.8 fusion.3
  108.7 0.0 copy-done.2
  108.7 1.5 fusion
  110.1 0.0 all-reduce.2.cloned.1.call-update
  110.2 1.3 copy.24
  111.5 73.2 %all-reduce.2.cloned.1.call-done = f32[512,256]{1,0:T(8,128)} async-done(((f32[512,256]{1,0:T(8,128)}), f32[512,256]{1,0:T(8,128)}) %all-reduce.2.cloned.1.call-update) | async-done | bytes 524304 | tf_op jit(solution)/shard_map/psum | solution.py:35
  184.7 2.1 %sub.3 = f32[512,256]{1,0:T(8,128)} subtract(f32[512,256]{1,0:T(8,128)} %param.6, f32[512,256]{1,0:T(8,128)} %all-reduce.2.cloned.1.call-done) | non-fusion elementwise | flops 131072 | bytes 1572864 | tf_op jit(solution)/shard_map/sub | solution.py:36
  (3 shorter events, 0.0 us)
Async XLA Ops:
  7.2 85.8 %copy-start = (bf16[512,2048]{1,0:T(8,128)(2,1)S(1)}, bf16[512,2048]{1,0:T(8,128)(2,1)}, u32[]{:S(2)}) copy-start(bf16[512,2048]{1,0:T(8,128)(2,1)} %param.4) | copy-start | bytes 6291460
  7.2 85.8 %all-gather.2.cloned.1.call-start = ((), (), s32[]{:S(2)}) async-start(), calls=%async_computation.2 | async-start | bytes 4718592 | tf_op jit(solution)/shard_map/all_gather | solution.py:24
  15.1 91.7 %reduce-scatter.2.cloned.1.call-start = ((), (), s32[]{:S(2)}) async-start(), calls=%async_computation.3 | async-start | bytes 3145728 | tf_op jit(solution)/shard_map/reduce_scatter | solution.py:27
  98.8 1.0 copy-start.1
  98.9 85.9 %all-reduce.2.cloned.1.call-start = ((), (), s32[]{:S(2)}) async-start(), calls=%async_computation.4 | async-start | bytes 1048576 | tf_op jit(solution)/shard_map/psum | solution.py:35
  106.8 1.8 copy-start.2
Sparse Core Ops, SparseCore 0:
  15.2 77.7 all-gather.1
  99.0 7.7 reduce-scatter.1
  111.2 73.4 all-reduce.1
where the time goes:
time: 194 us; the launch traced here: 193 us
  waiting for transfers between devices  155 us (80%)
  between operations  13.8 us (7%)
  matrix products  7.35 us (4%)
  local copies, waits for them, and re-layouts  7.1 us (4%)
  other arithmetic  5.29 us (3%)
  blocking collectives  4.15 us (2%)
    all_gather x1, waiting for transfers between devices, per_device(): lax.all_gather(swapped, 'prow', axis=0, tiled=True)  77.8 us
    psum x1, waiting for transfers between devices, per_device(): totals = lax.psum(diag_terms, 'prow')  73.2 us
    dot_general x1, matrix products, per_device(): jnp.dot(ancestor_inverse, lax.all_gather(swapped, 'prow', axis=0, tiled=T...  5.87 us
    reduce_scatter x1, waiting for transfers between devices, per_device(): lax.psum_scatter(partial_sum, 'pcol', scatter_dimension=1, tiled=True)  4.38 us
    all_to_all x1, blocking collectives, per_device(): lax.all_to_all(masked, 'pcol', split_axis=0, concat_axis=1, tiled=True)  4.15 us
  transfers between devices with their start and end apart: 3, of which 3 were waited for; matrix products, arithmetic and copies ran while one was open for 2% of the time, Pallas kernels for 0%

commit v1 on v0

v1 whole, which is shorter than its diff:
```python
import functools

import jax
import jax.numpy as jnp
from jax import lax
from jax.experimental import pallas as pl
from jax.experimental.pallas import tpu as pltpu
from jax.sharding import PartitionSpec as P

MESH = pl.DeviceIdType.MESH
NY = 2
N_COL = 2
NH = 2
SKEW = 2


def kernel(cfg, a_hbm, l_ref, d_ref, pat, out_ref, diag_ref, a_full, own, ubuf, dbuf, sd, su, fin, yin, acc,
           part, yr, ysum, zr, tot, ytot, a_sem, ph_ss, ph_rs, sd_ss, u_rs, su_ss, d_rs, fin_ss, y_rs, r_sem, zs_ss, zs_rs,
           zg_ss, zg_rs):
    nz, rt, share, na, s_n, b = cfg
    bh = b // NH
    tz = rt * NY
    row = lax.axis_index("prow")
    c = lax.axis_index("pcol")
    y = lax.rem(row, NY)
    z = row // NY
    oy = NY - 1 - y
    ypeer = {"prow": z * NY + oy}
    cpeer = {"pcol": 1 - c}

    def zdev(zz):
        return {"prow": zz * NY + y}

    barrier = pltpu.get_barrier_semaphore()
    pl.semaphore_signal(barrier, inc=1, device_id=ypeer, device_id_type=MESH)
    pl.semaphore_signal(barrier, inc=1, device_id=cpeer, device_id_type=MESH)
    for d in range(1, nz):
        pl.semaphore_signal(barrier, inc=1, device_id=zdev(lax.rem(z + d, nz)), device_id_type=MESH)
    acc[...] = jnp.zeros_like(acc)
    n_a = na // N_COL

    def a_local(i):
        return pltpu.make_async_copy(a_hbm.at[:, i * b:(i + 1) * b], a_full.at[c, i], a_sem.at[0, i])

    for i in range(n_a):
        a_local(i).start()
    pl.semaphore_wait(barrier, nz + 1)

    def remote(src, dst, ss, rs, dev):
        return pltpu.make_async_remote_copy(src_ref=src, dst_ref=dst, send_sem=ss, recv_sem=rs, device_id=dev,
                                            device_id_type=MESH)

    def a_send(i):
        return remote(a_hbm.at[:, i * b:(i + 1) * b], a_full.at[c, i], a_sem.at[1, i], a_sem.at[2, i], cpeer)

    def phase1(h, i):
        lanes = pl.ds(pl.multiple_of(oy * b + h * bh, 128), bh)
        return remote(l_ref.at[i * b:(i + 1) * b, lanes], own.at[h, y * rt + i], ph_ss.at[h, i], ph_rs.at[h, i], ypeer)

    for h in range(NH):
        for i in range(rt):
            phase1(h, i).start()
    for i in range(n_a):
        a_send(i).start()
    for h in range(NH):
        lanes = pl.ds(pl.multiple_of(y * b + h * bh, 128), bh)
        for i in range(rt):
            own[h, y * rt + i] = l_ref[i * b:(i + 1) * b, lanes]
    for i in range(rt):
        phase1(0, i).wait_recv()

    below = lax.rem(z + nz - 1, nz)
    above = lax.rem(z + 1, nz)

    def down(h, j):
        return remote(sd.at[h, j], ubuf.at[h, j], sd_ss.at[h, j], u_rs.at[h, j], zdev(below))

    def up(h, j):
        return remote(su.at[h, j], dbuf.at[h, j], su_ss.at[h, j], d_rs.at[h, j], zdev(above))

    def across(h, j):
        return remote(fin.at[h, j], yin.at[h, j], fin_ss.at[h, j], y_rs.at[h, j], ypeer)

    nodes = l_ref.shape[1] // b
    zc = min((na - s_n) // tz, nz - 1)
    j0 = jnp.maximum(tz * z - (na - s_n), 0)
    lag_d = SKEW * jnp.maximum(zc - z, 0)
    lag_u = SKEW * z
    lag_f = jnp.maximum(lag_d, lag_u)
    total = NH * s_n

    def tile_of(k, j):
        return pat[c * nodes + k, j]

    def own_tile(h, t):
        v = own[h, 0]
        for i in range(1, tz):
            v = lax.select(t == tz * z + i, own[h, i], v)
        return v

    def a_tile(t):
        part_at = lax.rem(t, rt) // share
        li = (t // rt) * share + lax.rem(t, share)
        return a_full[part_at, li]

    def step(s, carry):
        @pl.when(s == s_n)
        def _():
            for h in range(1, NH):
                for i in range(rt):
                    phase1(h, i).wait_recv()

        @pl.when(s == SKEW)
        def _():
            for i in range(n_a):
                a_local(i).wait()
                a_send(i).wait()

        pd = s - lag_d
        hd, jd = pd // s_n, j0 + lax.rem(pd, s_n)
        live = (pd >= 0) & (pd < total) & (jd < s_n)

        @pl.when(live & (z < nz - 1) & (jd + (na - s_n) >= tz * (z + 1)))
        def _():
            down(hd, jd).wait_recv()

        @pl.when(live & (z > 0))
        def _():
            t = tile_of(y, jd)
            sd[hd, jd] = lax.select(t < tz * (z + 1), own_tile(hd, t), ubuf[hd, jd])
            down(hd, jd).start()

        pu = s - lag_u
        hu, ju = pu // s_n, lax.rem(pu, s_n)
        live_u = (pu >= 0) & (pu < total) & (ju < s_n - 1)

        @pl.when(live_u & (z > 0) & (ju < tz * z))
        def _():
            up(hu, ju).wait_recv()

        @pl.when(live_u & (z < nz - 1) & (ju < tz * (z + 1)))
        def _():
            t = tile_of(y, ju)
            su[hu, ju] = lax.select(t >= tz * z, own_tile(hu, t), dbuf[hu, ju])
            up(hu, ju).start()

        pf = s - lag_f
        hf, jf = pf // s_n, lax.rem(pf, s_n)

        @pl.when((pf >= 0) & (pf < total))
        def _():
            t = tile_of(y, jf)
            v = lax.select(t < tz * z, dbuf[hf, jf], own_tile(hf, t))
            v = lax.select(t >= tz * (z + 1), ubuf[hf, jf], v)
            fin[hf, jf] = v
            across(hf, jf).start()
            acc[y, hf] += jnp.dot(a_tile(t), v, preferred_element_type=jnp.float32)

        py = pf - SKEW
        hy, jy = py // s_n, lax.rem(py, s_n)

        @pl.when((py >= 0) & (py < total))
        def _():
            across(hy, jy).wait_recv()
            t = tile_of(oy, jy)
            acc[oy, hy] += jnp.dot(a_tile(t), yin[hy, jy], preferred_element_type=jnp.float32)

        return carry

    lax.fori_loop(0, total + SKEW * nz, step, 0)

    for k in range(nodes):
        for i in range(rt):
            t = row * rt + i
            hit = pat[c * nodes + k, 0] == t
            for j in range(1, s_n):
                hit = hit | (pat[c * nodes + k, j] == t)
            m = -jnp.where(hit, 1.0, 0.0).astype(jnp.float32)
            for h in range(NH):
                out_ref[i * b:(i + 1) * b, k * b + h * bh:k * b + (h + 1) * bh] = acc[k, h, i * b:(i + 1) * b, :] * m
        x = out_ref[:, k * b:(k + 1) * b]
        hi = x.astype(jnp.bfloat16)
        lo = (x - hi.astype(jnp.float32)).astype(jnp.bfloat16)
        lk = l_ref[:, k * b:(k + 1) * b]
        dims = (((0,), (0,)), ((), ()))
        part[k] = lax.dot_general(lk, hi, dims, preferred_element_type=jnp.float32) + lax.dot_general(
            lk, lo, dims, preferred_element_type=jnp.float32)

    first = remote(part.at[oy], yr, r_sem.at[0], r_sem.at[1], ypeer)
    first.start()
    first.wait()
    ysum[...] = part[y] + yr[...]
    ch = b // nz

    def rs(d, src):
        to = lax.rem(z + d, nz)
        return remote(ysum.at[pl.ds(pl.multiple_of(to * ch, 8), ch), :], zr.at[d], zs_ss.at[d], zs_rs.at[d], zdev(to))

    for d in range(1, nz):
        rs(d, z).start()
    mine = pl.ds(pl.multiple_of(z * ch, 8), ch)
    total_z = ysum[mine, :]
    for d in range(1, nz):
        rs(d, z).wait_recv()
        total_z = total_z + zr[d]
    tot[mine, :] = total_z

    def ag(d):
        to = lax.rem(z + d, nz)
        return remote(tot.at[mine, :], tot.at[mine, :], zg_ss.at[d], zg_rs.at[d], zdev(to))

    def ag_in(d):
        at = lax.rem(z + nz - d, nz)
        there = pl.ds(pl.multiple_of(at * ch, 8), ch)
        return remote(tot.at[there, :], tot.at[there, :], zg_ss.at[d], zg_rs.at[d], zdev(at))

    for d in range(1, nz):
        ag(d).start()
    for d in range(1, nz):
        ag_in(d).wait_recv()
    last = remote(tot, ytot, r_sem.at[2], r_sem.at[3], ypeer)
    last.start()
    at_y = pl.ds(pl.multiple_of(y * b, 8), b)
    at_o = pl.ds(pl.multiple_of(oy * b, 8), b)
    diag_ref[at_y, :] = d_ref[at_y, :] - tot[...]

    for h in range(NH):
        for i in range(rt):
            phase1(h, i).wait_send()

    def drain(p, carry):
        h, j = p // s_n, lax.rem(p, s_n)

        @pl.when((z > 0) & (j >= j0))
        def _():
            down(h, j).wait_send()

        @pl.when((z < nz - 1) & (j < s_n - 1) & (j < tz * (z + 1)))
        def _():
            up(h, j).wait_send()

        across(h, j).wait_send()
        return carry

    lax.fori_loop(0, total, drain, 0)
    for d in range(1, nz):
        rs(d, z).wait_send()
        ag(d).wait_send()
    last.wait()
    diag_ref[at_o, :] = d_ref[at_o, :] - ytot[...]


def solution(mesh):
    n_row, n_col = mesh.shape["prow"], mesh.shape["pcol"]
    nz = n_row // NY

    def per_device(ancestor_inverse, l_panel, diag_inverse, pattern):
        b = diag_inverse.shape[1]
        rt = l_panel.shape[0] // b
        nodes = l_panel.shape[1] // b
        na, s_n = rt * n_row, pattern.shape[1]
        share = rt // n_col
        bh = b // NH
        bf, f32 = jnp.bfloat16, jnp.float32
        slots = pltpu.VMEM((NH, s_n, b, bh), bf)
        sems = pltpu.SemaphoreType.DMA((NH, s_n))
        zsem = pltpu.SemaphoreType.DMA((nz,))
        vmem = pl.BlockSpec(memory_space=pltpu.VMEM)
        return pl.pallas_call(
            functools.partial(kernel, (nz, rt, share, na, s_n, b)),
            out_shape=(jax.ShapeDtypeStruct(l_panel.shape, f32), jax.ShapeDtypeStruct(diag_inverse.shape, f32)),
            in_specs=[pl.BlockSpec(memory_space=pl.ANY), vmem, vmem, pl.BlockSpec(memory_space=pltpu.SMEM)],
            out_specs=(vmem, vmem),
            scratch_shapes=[
                pltpu.VMEM((n_col, na // n_col, rt * b, b), bf),
                pltpu.VMEM((NH, rt * NY, b, bh), bf),
                slots, slots, slots, slots, slots, slots,
                pltpu.VMEM((nodes, NH, rt * b, bh), f32),
                pltpu.VMEM((nodes, b, b), f32),
                pltpu.VMEM((b, b), f32),
                pltpu.VMEM((b, b), f32),
                pltpu.VMEM((nz, b // nz, b), f32),
                pltpu.VMEM((b, b), f32),
                pltpu.VMEM((b, b), f32),
                pltpu.SemaphoreType.DMA((3, na // n_col)),
                pltpu.SemaphoreType.DMA((NH, rt)),
                pltpu.SemaphoreType.DMA((NH, rt)),
                sems, sems, sems, sems, sems, sems,
                pltpu.SemaphoreType.DMA((4,)),
                zsem, zsem, zsem, zsem,
            ],
            compiler_params=pltpu.CompilerParams(collective_id=0, has_side_effects=True, vmem_limit_bytes=56 * 2**20),
            cost_estimate=pl.CostEstimate(flops=4 * 10**9, bytes_accessed=2**23, transcendentals=0),
        )(ancestor_inverse, l_panel, diag_inverse, pattern)

    return jax.shard_map(
        per_device,
        mesh=mesh,
        in_specs=(P(("pole", "prow"), "pcol"), P(("pole", "prow"), "pcol"), P(("pole", "pcol"), None), P()),
        out_specs=(P(("pole", "prow"), "pcol"), P(("pole", "pcol"), None)),
        check_vma=False,
    )
```

time: 194 us -> 77 us (0.40)
  waiting for transfers between devices: 155 us -> 0 us
  Pallas kernels: 0 us -> 73.1 us
  between operations: 13.8 us -> 0.65 us
  matrix products: 7.35 us -> 0 us
  other arithmetic: 5.29 us -> 0 us
  blocking collectives: 4.15 us -> 0 us
  local copies, waits for them, and re-layouts: 7.1 us -> 3.12 us
    all_gather x1 -> x0, waiting for transfers between devices: 77.8 us -> none  [per_device(): lax.all_gather(swapped, 'prow', axis=0, tiled=True)]
    psum x1 -> x0, waiting for transfers between devices: 73.2 us -> none  [per_device(): totals = lax.psum(diag_terms, 'prow')]
    pallas_call x0 -> x1, Pallas kernels: none -> 73.1 us  [per_device(): pl.pallas_call(functools.partial(kernel, (nz, rt, share, na, s_n, b)), ou...]
    dot_general x2 -> x0, matrix products: 7.35 us -> none  [the longest x1 5.87 us: per_device(): jnp.dot(ancestor_inverse, lax.all_gather(swapped, 'prow', axis=0, tiled=T...]
    reduce_scatter x1 -> x0, waiting for transfers between devices: 4.38 us -> none  [per_device(): lax.psum_scatter(partial_sum, 'pcol', scatter_dimension=1, tiled=True)]
    all_to_all x1 -> x0, blocking collectives: 4.15 us -> none  [per_device(): lax.all_to_all(masked, 'pcol', split_axis=0, concat_axis=1, tiled=True)]
    sub x1 -> x0, other arithmetic: 2.06 us -> none  [per_device(): diag_blocks = diag_inverse - totals.reshape(local_nodes * B, B)]
  transfers between devices with their start and end apart: 3 -> 0, of which waited for: 3 -> 0; matrix products, arithmetic and copies ran while one was open for 2% -> 0% of each run, Pallas kernels for 0% -> 0%
where the time goes in v1:
time: 77 us; the launch traced here: 76.9 us
  Pallas kernels  73.1 us (95%)
  local copies, waits for them, and re-layouts  3.12 us (4%)
    pallas_call x1, Pallas kernels, per_device(): pl.pallas_call(functools.partial(kernel, (nz, rt, share, na, s_n, b)), ou...  73.1 us
    unnamed x4, local copies, waits for them, and re-layouts  3.12 us

profile of v1, /device:TPU:0, one launch (start us, length us, event | category | flops | bytes accessed | tf_op | source)
XLA Modules:
  0.0 76.9 jit_solution(10854358701501522470)
XLA Ops:
  0.6 73.1 %shard_map.59 = (f32[512,512]{1,0:T(8,128)}, f32[512,256]{1,0:T(8,128)}) custom-call(bf16[512,2048]{1,0:T(8,128)(2,1)} %a_hbm.1, bf16[512,512]{1,0:T(8,128)(2,1)} %l_ref.1, f32[512,256]{1,0:T(8,128)} %d_ref.1, s32[4,8]{1,0:T(4,128)} %pat.1), custom_call_target="tpu_custom_call" | custom-call | flops 4000000000 | bytes 8388608 | tf_op jit(solution)/shard_map/pallas_call | solution.py:269
  73.8 0.0 copy-start
  73.8 2.3 %copy.8 = f32[512,512]{1,0:T(8,128)} copy(f32[512,512]{1,0:T(8,128)} %get-tuple-element.4) | data formatting | bytes 2097152
  76.1 0.0 copy-done
  76.1 0.8 %copy.9 = f32[512,256]{1,0:T(8,128)} copy(f32[512,256]{1,0:T(8,128)S(1)} %copy-done) | data formatting | bytes 1048576
Async XLA Ops:
  73.8 2.3 %copy-start = (f32[512,256]{1,0:T(8,128)S(1)}, f32[512,256]{1,0:T(8,128)}, u32[]{:S(2)}) copy-start(f32[512,256]{1,0:T(8,128)} %get-tuple-element.5) | copy-start | bytes 1572868

commit v2 on v1

--- a/solution.py
+++ b/solution.py
@@ -11,6 +11,7 @@
 NY = 2
 N_COL = 2
 NH = 2
+GAP = 3
 SKEW = 2
 
 
@@ -103,6 +104,76 @@
         li = (t // rt) * share + lax.rem(t, share)
         return a_full[part_at, li]
 
+    ch = b // nz
+    at_y = pl.ds(pl.multiple_of(y * b, 8), b)
+    at_o = pl.ds(pl.multiple_of(oy * b, 8), b)
+    mine = pl.ds(pl.multiple_of(z * ch, 8), ch)
+
+    def first(h):
+        return remote(part.at[h, oy], yr.at[h], r_sem.at[h, 0], r_sem.at[h, 1], ypeer)
+
+    def last(h):
+        return remote(tot.at[h], ytot.at[h], r_sem.at[h, 2], r_sem.at[h, 3], ypeer)
+
+    def rs(h, d):
+        to = lax.rem(z + d, nz)
+        return remote(ysum.at[h, pl.ds(pl.multiple_of(to * ch, 8), ch), :], zr.at[h, d], zs_ss.at[h, d],
+                      zs_rs.at[h, d], zdev(to))
+
+    def ag(h, d):
+        to = lax.rem(z + d, nz)
+        return remote(tot.at[h, mine, :], tot.at[h, mine, :], zg_ss.at[h, d], zg_rs.at[h, d], zdev(to))
+
+    def ag_in(h, d):
+        at = lax.rem(z + nz - d, nz)
+        there = pl.ds(pl.multiple_of(at * ch, 8), ch)
+        return remote(tot.at[h, there, :], tot.at[h, there, :], zg_ss.at[h, d], zg_rs.at[h, d], zdev(at))
+
+    def reduce_0(h):
+        for k in range(nodes):
+            at = slice(k * b + h * bh, k * b + (h + 1) * bh)
+            for i in range(rt):
+                t = row * rt + i
+                hit = pat[c * nodes + k, 0] == t
+                for j in range(1, s_n):
+                    hit = hit | (pat[c * nodes + k, j] == t)
+                m = -jnp.where(hit, 1.0, 0.0).astype(jnp.float32)
+                out_ref[i * b:(i + 1) * b, at] = acc[k, h, i * b:(i + 1) * b, :] * m
+            x = out_ref[:, at]
+            hi = x.astype(jnp.bfloat16)
+            lo = (x - hi.astype(jnp.float32)).astype(jnp.bfloat16)
+            both = lax.dot_general(l_ref[:, k * b:(k + 1) * b], jnp.concatenate([hi, lo], axis=1),
+                                   (((0,), (0,)), ((), ())), preferred_element_type=jnp.float32)
+            part[h, k] = both[:, :bh] + both[:, bh:]
+        first(h).start()
+
+    def reduce_1(h):
+        first(h).wait()
+        ysum[h] = part[h, y] + yr[h]
+        for d in range(1, nz):
+            rs(h, d).start()
+
+    def reduce_2(h):
+        total_z = ysum[h, mine, :]
+        for d in range(1, nz):
+            rs(h, d).wait_recv()
+            total_z = total_z + zr[h, d]
+        tot[h, mine, :] = total_z
+        for d in range(1, nz):
+            ag(h, d).start()
+
+    def reduce_3(h):
+        for d in range(1, nz):
+            ag_in(h, d).wait_recv()
+        last(h).start()
+        lanes = slice(h * bh, (h + 1) * bh)
+        diag_ref[at_y, lanes] = d_ref[at_y, lanes] - tot[h]
+
+    def reduce_4(h):
+        lanes = slice(h * bh, (h + 1) * bh)
+        last(h).wait_recv()
+        diag_ref[at_o, lanes] = d_ref[at_o, lanes] - ytot[h]
+
     def step(s, carry):
         @pl.when(s == s_n)
         def _():
@@ -165,89 +236,60 @@
             t = tile_of(oy, jy)
             acc[oy, hy] += jnp.dot(a_tile(t), yin[hy, jy], preferred_element_type=jnp.float32)
 
+        for h in range(NH - 1):
+            done = (h + 1) * s_n + SKEW
+
+            @pl.when(s == done + lag_f)
+            def _(h=h):
+                reduce_0(h)
+
+            @pl.when(s == done + lag_f + GAP)
+            def _(h=h):
+                reduce_1(h)
+
+            @pl.when(s == done + SKEW * (nz - 1) + 2 * GAP)
+            def _(h=h):
+                reduce_2(h)
+
         return carry
 
     lax.fori_loop(0, total + SKEW * nz, step, 0)
 
-    for k in range(nodes):
+    for h in range(NH - 1):
+        reduce_3(h)
+    h = NH - 1
+    reduce_0(h)
+    for g in range(NH - 1):
+        reduce_4(g)
+    reduce_1(h)
+    reduce_2(h)
+    reduce_3(h)
+
+    for g in range(NH):
         for i in range(rt):
-            t = row * rt + i
-            hit = pat[c * nodes + k, 0] == t
-            for j in range(1, s_n):
-                hit = hit | (pat[c * nodes + k, j] == t)
-            m = -jnp.where(hit, 1.0, 0.0).astype(jnp.float32)
-            for h in range(NH):
-                out_ref[i * b:(i + 1) * b, k * b + h * bh:k * b + (h + 1) * bh] = acc[k, h, i * b:(i + 1) * b, :] * m
-        x = out_ref[:, k * b:(k + 1) * b]
-        hi = x.astype(jnp.bfloat16)
-        lo = (x - hi.astype(jnp.float32)).astype(jnp.bfloat16)
-        lk = l_ref[:, k * b:(k + 1) * b]
-        dims = (((0,), (0,)), ((), ()))
-        part[k] = lax.dot_general(lk, hi, dims, preferred_element_type=jnp.float32) + lax.dot_general(
-            lk, lo, dims, preferred_element_type=jnp.float32)
-
-    first = remote(part.at[oy], yr, r_sem.at[0], r_sem.at[1], ypeer)
-    first.start()
-    first.wait()
-    ysum[...] = part[y] + yr[...]
-    ch = b // nz
-
-    def rs(d, src):
-        to = lax.rem(z + d, nz)
-        return remote(ysum.at[pl.ds(pl.multiple_of(to * ch, 8), ch), :], zr.at[d], zs_ss.at[d], zs_rs.at[d], zdev(to))
-
-    for d in range(1, nz):
-        rs(d, z).start()
-    mine = pl.ds(pl.multiple_of(z * ch, 8), ch)
-    total_z = ysum[mine, :]
-    for d in range(1, nz):
-        rs(d, z).wait_recv()
-        total_z = total_z + zr[d]
-    tot[mine, :] = total_z
-
-    def ag(d):
-        to = lax.rem(z + d, nz)
-        return remote(tot.at[mine, :], tot.at[mine, :], zg_ss.at[d], zg_rs.at[d], zdev(to))
-
-    def ag_in(d):
-        at = lax.rem(z + nz - d, nz)
-        there = pl.ds(pl.multiple_of(at * ch, 8), ch)
-        return remote(tot.at[there, :], tot.at[there, :], zg_ss.at[d], zg_rs.at[d], zdev(at))
-
-    for d in range(1, nz):
-        ag(d).start()
-    for d in range(1, nz):
-        ag_in(d).wait_recv()
-    last = remote(tot, ytot, r_sem.at[2], r_sem.at[3], ypeer)
-    last.start()
-    at_y = pl.ds(pl.multiple_of(y * b, 8), b)
-    at_o = pl.ds(pl.multiple_of(oy * b, 8), b)
-    diag_ref[at_y, :] = d_ref[at_y, :] - tot[...]
-
-    for h in range(NH):
-        for i in range(rt):
-            phase1(h, i).wait_send()
+            phase1(g, i).wait_send()
 
     def drain(p, carry):
-        h, j = p // s_n, lax.rem(p, s_n)
+        g, j = p // s_n, lax.rem(p, s_n)
 
         @pl.when((z > 0) & (j >= j0))
         def _():
-            down(h, j).wait_send()
+            down(g, j).wait_send()
 
         @pl.when((z < nz - 1) & (j < s_n - 1) & (j < tz * (z + 1)))
         def _():
-            up(h, j).wait_send()
-
-        across(h, j).wait_send()
+            up(g, j).wait_send()
+
+        across(g, j).wait_send()
         return carry
 
     lax.fori_loop(0, total, drain, 0)
-    for d in range(1, nz):
-        rs(d, z).wait_send()
-        ag(d).wait_send()
-    last.wait()
-    diag_ref[at_o, :] = d_ref[at_o, :] - ytot[...]
+    for g in range(NH):
+        for d in range(1, nz):
+            rs(g, d).wait_send()
+            ag(g, d).wait_send()
+        last(g).wait_send()
+    reduce_4(h)
 
 
 def solution(mesh):
@@ -264,7 +306,8 @@
         bf, f32 = jnp.bfloat16, jnp.float32
         slots = pltpu.VMEM((NH, s_n, b, bh), bf)
         sems = pltpu.SemaphoreType.DMA((NH, s_n))
-        zsem = pltpu.SemaphoreType.DMA((nz,))
+        zsem = pltpu.SemaphoreType.DMA((NH, nz))
+        half = pltpu.VMEM((NH, b, bh), f32)
         vmem = pl.BlockSpec(memory_space=pltpu.VMEM)
         return pl.pallas_call(
             functools.partial(kernel, (nz, rt, share, na, s_n, b)),
@@ -276,17 +319,15 @@
                 pltpu.VMEM((NH, rt * NY, b, bh), bf),
                 slots, slots, slots, slots, slots, slots,
                 pltpu.VMEM((nodes, NH, rt * b, bh), f32),
-                pltpu.VMEM((nodes, b, b), f32),
-                pltpu.VMEM((b, b), f32),
-                pltpu.VMEM((b, b), f32),
-                pltpu.VMEM((nz, b // nz, b), f32),
-                pltpu.VMEM((b, b), f32),
-                pltpu.VMEM((b, b), f32),
+                pltpu.VMEM((NH, nodes, b, bh), f32),
+                half, half,
+                pltpu.VMEM((NH, nz, b // nz, bh), f32),
+                half, half,
                 pltpu.SemaphoreType.DMA((3, na // n_col)),
                 pltpu.SemaphoreType.DMA((NH, rt)),
                 pltpu.SemaphoreType.DMA((NH, rt)),
                 sems, sems, sems, sems, sems, sems,
-                pltpu.SemaphoreType.DMA((4,)),
+                pltpu.SemaphoreType.DMA((NH, 4)),
                 zsem, zsem, zsem, zsem,
             ],
             compiler_params=pltpu.CompilerParams(collective_id=0, has_side_effects=True, vmem_limit_bytes=56 * 2**20),

time: 77 us -> 79.8 us (1.036)
  Pallas kernels: 73.1 us -> 75.9 us
    pallas_call x1, Pallas kernels: 73.1 us -> 75.9 us  [per_device(): pl.pallas_call(functools.partial(kernel, (nz, rt, share, na, s_n, b)), ou...]
where the time goes in v2:
time: 79.8 us; the launch traced here: 79.6 us
  Pallas kernels  75.9 us (95%)
  local copies, waits for them, and re-layouts  3.12 us (4%)
    pallas_call x1, Pallas kernels, per_device(): pl.pallas_call(functools.partial(kernel, (nz, rt, share, na, s_n, b)), ou...  75.9 us
    unnamed x4, local copies, waits for them, and re-layouts  3.12 us

profile of v2, /device:TPU:0, one launch (start us, length us, event | category | flops | bytes accessed | tf_op | source)
XLA Modules:
  0.0 79.6 jit_solution(10484985029203260163)
XLA Ops:
  0.6 75.9 %shard_map.59 = (f32[512,512]{1,0:T(8,128)}, f32[512,256]{1,0:T(8,128)}) custom-call(bf16[512,2048]{1,0:T(8,128)(2,1)} %a_hbm.1, bf16[512,512]{1,0:T(8,128)(2,1)} %l_ref.1, f32[512,256]{1,0:T(8,128)} %d_ref.1, s32[4,8]{1,0:T(4,128)} %pat.1), custom_call_target="tpu_custom_call" | custom-call | flops 4000000000 | bytes 8388608 | tf_op jit(solution)/shard_map/pallas_call | solution.py:312
  76.5 0.0 copy-start
  76.5 2.3 %copy.8 = f32[512,512]{1,0:T(8,128)} copy(f32[512,512]{1,0:T(8,128)} %get-tuple-element.4) | data formatting | bytes 2097152
  78.8 0.0 copy-done
  78.8 0.8 copy.9
Async XLA Ops:
  76.5 2.3 %copy-start = (f32[512,256]{1,0:T(8,128)S(1)}, f32[512,256]{1,0:T(8,128)}, u32[]{:S(2)}) copy-start(f32[512,256]{1,0:T(8,128)} %get-tuple-element.5) | copy-start | bytes 1572868

commit v3 on v2

--- a/solution.py
+++ b/solution.py
@@ -12,7 +12,7 @@
 N_COL = 2
 NH = 2
 GAP = 3
-SKEW = 2
+SKEW = 4
 
 
 def kernel(cfg, a_hbm, l_ref, d_ref, pat, out_ref, diag_ref, a_full, own, ubuf, dbuf, sd, su, fin, yin, acc,
@@ -181,7 +181,7 @@
                 for i in range(rt):
                     phase1(h, i).wait_recv()
 
-        @pl.when(s == SKEW)
+        @pl.when(s == lag_f)
         def _():
             for i in range(n_a):
                 a_local(i).wait()

time: 79.8 us -> 77 us (0.965)
  Pallas kernels: 75.9 us -> 73.1 us
    pallas_call x1, Pallas kernels: 75.9 us -> 73.1 us  [per_device(): pl.pallas_call(functools.partial(kernel, (nz, rt, share, na, s_n, b)), ou...]
where the time goes in v3:
time: 77 us; the launch traced here: 76.8 us
  Pallas kernels  73.1 us (95%)
  local copies, waits for them, and re-layouts  3.12 us (4%)
    pallas_call x1, Pallas kernels, per_device(): pl.pallas_call(functools.partial(kernel, (nz, rt, share, na, s_n, b)), ou...  73.1 us
    unnamed x4, local copies, waits for them, and re-layouts  3.12 us

profile of v3, /device:TPU:0, one launch (start us, length us, event | category | flops | bytes accessed | tf_op | source)
XLA Modules:
  0.0 76.8 jit_solution(5656333986746075565)
XLA Ops:
  0.6 73.1 %shard_map.59 = (f32[512,512]{1,0:T(8,128)}, f32[512,256]{1,0:T(8,128)}) custom-call(bf16[512,2048]{1,0:T(8,128)(2,1)} %a_hbm.1, bf16[512,512]{1,0:T(8,128)(2,1)} %l_ref.1, f32[512,256]{1,0:T(8,128)} %d_ref.1, s32[4,8]{1,0:T(4,128)} %pat.1), custom_call_target="tpu_custom_call" | custom-call | flops 4000000000 | bytes 8388608 | tf_op jit(solution)/shard_map/pallas_call | solution.py:312
  73.7 0.0 copy-start
  73.7 2.3 %copy.8 = f32[512,512]{1,0:T(8,128)} copy(f32[512,512]{1,0:T(8,128)} %get-tuple-element.4) | data formatting | bytes 2097152
  76.0 0.0 copy-done
  76.1 0.8 %copy.9 = f32[512,256]{1,0:T(8,128)} copy(f32[512,256]{1,0:T(8,128)S(1)} %copy-done) | data formatting | bytes 1048576
Async XLA Ops:
  73.7 2.3 %copy-start = (f32[512,256]{1,0:T(8,128)S(1)}, f32[512,256]{1,0:T(8,128)}, u32[]{:S(2)}) copy-start(f32[512,256]{1,0:T(8,128)} %get-tuple-element.5) | copy-start | bytes 1572868

commit v4 on v3

--- a/solution.py
+++ b/solution.py
@@ -10,9 +10,9 @@
 MESH = pl.DeviceIdType.MESH
 NY = 2
 N_COL = 2
-NH = 2
+NH = 1
 GAP = 3
-SKEW = 4
+SKEW = 2
 
 
 def kernel(cfg, a_hbm, l_ref, d_ref, pat, out_ref, diag_ref, a_full, own, ubuf, dbuf, sd, su, fin, yin, acc,

time: 77 us -> 77.2 us (level)
  no operation moved by 1% of the time
where the time goes in v4:
time: 77.2 us; the launch traced here: 77 us
  Pallas kernels  73.2 us (95%)
  local copies, waits for them, and re-layouts  3.12 us (4%)
    pallas_call x1, Pallas kernels, per_device(): pl.pallas_call(functools.partial(kernel, (nz, rt, share, na, s_n, b)), ou...  73.2 us
    unnamed x4, local copies, waits for them, and re-layouts  3.12 us

profile of v4, /device:TPU:0, one launch (start us, length us, event | category | flops | bytes accessed | tf_op | source)
XLA Modules:
  0.0 77.0 jit_solution(4039594223999873988)
XLA Ops:
  0.6 73.2 %shard_map.59 = (f32[512,512]{1,0:T(8,128)}, f32[512,256]{1,0:T(8,128)}) custom-call(bf16[512,2048]{1,0:T(8,128)(2,1)} %a_hbm.1, bf16[512,512]{1,0:T(8,128)(2,1)} %l_ref.1, f32[512,256]{1,0:T(8,128)} %d_ref.1, s32[4,8]{1,0:T(4,128)} %pat.1), custom_call_target="tpu_custom_call" | custom-call | flops 4000000000 | bytes 8388608 | tf_op jit(solution)/shard_map/pallas_call | solution.py:312
  73.9 0.0 copy-start
  73.9 2.3 %copy.8 = f32[512,512]{1,0:T(8,128)} copy(f32[512,512]{1,0:T(8,128)} %get-tuple-element.4) | data formatting | bytes 2097152
  76.2 0.0 copy-done
  76.2 0.8 %copy.9 = f32[512,256]{1,0:T(8,128)} copy(f32[512,256]{1,0:T(8,128)S(1)} %copy-done) | data formatting | bytes 1048576
Async XLA Ops:
  73.9 2.3 %copy-start = (f32[512,256]{1,0:T(8,128)S(1)}, f32[512,256]{1,0:T(8,128)}, u32[]{:S(2)}) copy-start(f32[512,256]{1,0:T(8,128)} %get-tuple-element.5) | copy-start | bytes 1572868

commit v5 on v3

--- a/solution.py
+++ b/solution.py
@@ -12,7 +12,7 @@
 N_COL = 2
 NH = 2
 GAP = 3
-SKEW = 4
+SKEW = 3
 
 
 def kernel(cfg, a_hbm, l_ref, d_ref, pat, out_ref, diag_ref, a_full, own, ubuf, dbuf, sd, su, fin, yin, acc,
@@ -52,7 +52,8 @@
                                             device_id_type=MESH)
 
     def a_send(i):
-        return remote(a_hbm.at[:, i * b:(i + 1) * b], a_full.at[c, i], a_sem.at[1, i], a_sem.at[2, i], cpeer)
+        cols = pl.ds(pl.multiple_of(i * b, 128), b)
+        return remote(a_hbm.at[:, cols], a_full.at[c, i], a_sem.at[1, i], a_sem.at[2, i], cpeer)
 
     def phase1(h, i):
         lanes = pl.ds(pl.multiple_of(oy * b + h * bh, 128), bh)
@@ -61,8 +62,6 @@
     for h in range(NH):
         for i in range(rt):
             phase1(h, i).start()
-    for i in range(n_a):
-        a_send(i).start()
     for h in range(NH):
         lanes = pl.ds(pl.multiple_of(y * b + h * bh, 128), bh)
         for i in range(rt):
@@ -103,6 +102,13 @@
         part_at = lax.rem(t, rt) // share
         li = (t // rt) * share + lax.rem(t, share)
         return a_full[part_at, li]
+
+    def bulk(k, src):
+        def one(j, carry):
+            acc[k, 0] += jnp.dot(a_tile(tile_of(k, j)), src[0, j], preferred_element_type=jnp.float32)
+            return carry
+
+        lax.fori_loop(0, s_n, one, 0)
 
     ch = b // nz
     at_y = pl.ds(pl.multiple_of(y * b, 8), b)
@@ -181,7 +187,7 @@
                 for i in range(rt):
                     phase1(h, i).wait_recv()
 
-        @pl.when(s == lag_f)
+        @pl.when(s == s_n + lag_f)
         def _():
             for i in range(n_a):
                 a_local(i).wait()
@@ -225,7 +231,14 @@
             v = lax.select(t >= tz * (z + 1), ubuf[hf, jf], v)
             fin[hf, jf] = v
             across(hf, jf).start()
-            acc[y, hf] += jnp.dot(a_tile(t), v, preferred_element_type=jnp.float32)
+
+            @pl.when(hf > 0)
+            def _():
+                acc[y, hf] += jnp.dot(a_tile(t), v, preferred_element_type=jnp.float32)
+
+        @pl.when(pf == s_n)
+        def _():
+            bulk(y, fin)
 
         py = pf - SKEW
         hy, jy = py // s_n, lax.rem(py, s_n)
@@ -234,7 +247,18 @@
         def _():
             across(hy, jy).wait_recv()
             t = tile_of(oy, jy)
-            acc[oy, hy] += jnp.dot(a_tile(t), yin[hy, jy], preferred_element_type=jnp.float32)
+
+            @pl.when(hy > 0)
+            def _():
+                acc[oy, hy] += jnp.dot(a_tile(t), yin[hy, jy], preferred_element_type=jnp.float32)
+
+        @pl.when(py == s_n)
+        def _():
+            bulk(oy, yin)
+
+        @pl.when(s < n_a)
+        def _():
+            a_send(s).start()
 
         for h in range(NH - 1):
             done = (h + 1) * s_n + SKEW

time: 77 us -> 77.7 us (level)
  no operation moved by 1% of the time
where the time goes in v5:
time: 77.7 us; the launch traced here: 77.5 us
  Pallas kernels  73.7 us (95%)
  local copies, waits for them, and re-layouts  3.12 us (4%)
    pallas_call x1, Pallas kernels, per_device(): pl.pallas_call(functools.partial(kernel, (nz, rt, share, na, s_n, b)), ou...  73.7 us
    unnamed x4, local copies, waits for them, and re-layouts  3.12 us

profile of v5, /device:TPU:0, one launch (start us, length us, event | category | flops | bytes accessed | tf_op | source)
XLA Modules:
  0.0 77.5 jit_solution(16440420563399501417)
XLA Ops:
  0.6 73.7 %shard_map.59 = (f32[512,512]{1,0:T(8,128)}, f32[512,256]{1,0:T(8,128)}) custom-call(bf16[512,2048]{1,0:T(8,128)(2,1)} %a_hbm.1, bf16[512,512]{1,0:T(8,128)(2,1)} %l_ref.1, f32[512,256]{1,0:T(8,128)} %d_ref.1, s32[4,8]{1,0:T(4,128)} %pat.1), custom_call_target="tpu_custom_call" | custom-call | flops 4000000000 | bytes 8388608 | tf_op jit(solution)/shard_map/pallas_call | solution.py:336
  74.4 0.0 copy-start
  74.4 2.3 %copy.8 = f32[512,512]{1,0:T(8,128)} copy(f32[512,512]{1,0:T(8,128)} %get-tuple-element.4) | data formatting | bytes 2097152
  76.7 0.0 copy-done
  76.7 0.8 %copy.9 = f32[512,256]{1,0:T(8,128)} copy(f32[512,256]{1,0:T(8,128)S(1)} %copy-done) | data formatting | bytes 1048576
Async XLA Ops:
  74.4 2.3 %copy-start = (f32[512,256]{1,0:T(8,128)S(1)}, f32[512,256]{1,0:T(8,128)}, u32[]{:S(2)}) copy-start(f32[512,256]{1,0:T(8,128)} %get-tuple-element.5) | copy-start | bytes 1572868

commit v6 on v3

--- a/solution.py
+++ b/solution.py
@@ -11,8 +11,7 @@
 NY = 2
 N_COL = 2
 NH = 2
-GAP = 3
-SKEW = 4
+SKEW = 3
 
 
 def kernel(cfg, a_hbm, l_ref, d_ref, pat, out_ref, diag_ref, a_full, own, ubuf, dbuf, sd, su, fin, yin, acc,
@@ -243,27 +242,18 @@
             def _(h=h):
                 reduce_0(h)
 
-            @pl.when(s == done + lag_f + GAP)
-            def _(h=h):
-                reduce_1(h)
-
-            @pl.when(s == done + SKEW * (nz - 1) + 2 * GAP)
-            def _(h=h):
-                reduce_2(h)
-
         return carry
 
     lax.fori_loop(0, total + SKEW * nz, step, 0)
 
-    for h in range(NH - 1):
-        reduce_3(h)
     h = NH - 1
+    for g in range(h):
+        reduce_1(g)
     reduce_0(h)
-    for g in range(NH - 1):
-        reduce_4(g)
-    reduce_1(h)
-    reduce_2(h)
-    reduce_3(h)
+    for phase, following in ((reduce_1, reduce_2), (reduce_2, reduce_3), (reduce_3, reduce_4)):
+        for g in range(h):
+            following(g)
+        phase(h)
 
     for g in range(NH):
         for i in range(rt):

time: 77 us -> 72.4 us (0.940)
  Pallas kernels: 73.1 us -> 68.5 us
    pallas_call x1, Pallas kernels: 73.1 us -> 68.5 us  [per_device(): pl.pallas_call(functools.partial(kernel, (nz, rt, share, na, s_n, b)), ou...]
where the time goes in v6:
time: 72.4 us; the launch traced here: 72.2 us
  Pallas kernels  68.5 us (95%)
  local copies, waits for them, and re-layouts  3.12 us (4%)
    pallas_call x1, Pallas kernels, per_device(): pl.pallas_call(functools.partial(kernel, (nz, rt, share, na, s_n, b)), ou...  68.5 us
    unnamed x4, local copies, waits for them, and re-layouts  3.12 us

profile of v6, /device:TPU:0, one launch (start us, length us, event | category | flops | bytes accessed | tf_op | source)
XLA Modules:
  0.0 72.2 jit_solution(4566851509891828457)
XLA Ops:
  0.6 68.5 %shard_map.59 = (f32[512,512]{1,0:T(8,128)}, f32[512,256]{1,0:T(8,128)}) custom-call(bf16[512,2048]{1,0:T(8,128)(2,1)} %a_hbm.1, bf16[512,512]{1,0:T(8,128)(2,1)} %l_ref.1, f32[512,256]{1,0:T(8,128)} %d_ref.1, s32[4,8]{1,0:T(4,128)} %pat.1), custom_call_target="tpu_custom_call" | custom-call | flops 4000000000 | bytes 8388608 | tf_op jit(solution)/shard_map/pallas_call | solution.py:302
  69.1 0.0 copy-start
  69.1 2.3 %copy.8 = f32[512,512]{1,0:T(8,128)} copy(f32[512,512]{1,0:T(8,128)} %get-tuple-element.4) | data formatting | bytes 2097152
  71.4 0.0 copy-done
  71.4 0.8 %copy.9 = f32[512,256]{1,0:T(8,128)} copy(f32[512,256]{1,0:T(8,128)S(1)} %copy-done) | data formatting | bytes 1048576
Async XLA Ops:
  69.1 2.3 %copy-start = (f32[512,256]{1,0:T(8,128)S(1)}, f32[512,256]{1,0:T(8,128)}, u32[]{:S(2)}) copy-start(f32[512,256]{1,0:T(8,128)} %get-tuple-element.5) | copy-start | bytes 1572868

commit v7 on v6

--- a/solution.py
+++ b/solution.py
@@ -11,7 +11,8 @@
 NY = 2
 N_COL = 2
 NH = 2
-SKEW = 3
+GAP = 5
+SKEW = 4
 
 
 def kernel(cfg, a_hbm, l_ref, d_ref, pat, out_ref, diag_ref, a_full, own, ubuf, dbuf, sd, su, fin, yin, acc,
@@ -242,13 +243,15 @@
             def _(h=h):
                 reduce_0(h)
 
+            @pl.when(s == done + lag_f + min(GAP, s_n - 1))
+            def _(h=h):
+                reduce_1(h)
+
         return carry
 
     lax.fori_loop(0, total + SKEW * nz, step, 0)
 
     h = NH - 1
-    for g in range(h):
-        reduce_1(g)
     reduce_0(h)
     for phase, following in ((reduce_1, reduce_2), (reduce_2, reduce_3), (reduce_3, reduce_4)):
         for g in range(h):

time: 72.4 us -> 71 us (0.981)
  Pallas kernels: 68.5 us -> 67.1 us
    pallas_call x1, Pallas kernels: 68.5 us -> 67.1 us  [per_device(): pl.pallas_call(functools.partial(kernel, (nz, rt, share, na, s_n, b)), ou...]
where the time goes in v7:
time: 71 us; the launch traced here: 70.9 us
  Pallas kernels  67.1 us (95%)
  local copies, waits for them, and re-layouts  3.12 us (4%)
    pallas_call x1, Pallas kernels, per_device(): pl.pallas_call(functools.partial(kernel, (nz, rt, share, na, s_n, b)), ou...  67.1 us
    unnamed x4, local copies, waits for them, and re-layouts  3.12 us

profile of v7, /device:TPU:0, one launch (start us, length us, event | category | flops | bytes accessed | tf_op | source)
XLA Modules:
  0.0 70.9 jit_solution(693862489965622742)
XLA Ops:
  0.6 67.1 %shard_map.59 = (f32[512,512]{1,0:T(8,128)}, f32[512,256]{1,0:T(8,128)}) custom-call(bf16[512,2048]{1,0:T(8,128)(2,1)} %a_hbm.1, bf16[512,512]{1,0:T(8,128)(2,1)} %l_ref.1, f32[512,256]{1,0:T(8,128)} %d_ref.1, s32[4,8]{1,0:T(4,128)} %pat.1), custom_call_target="tpu_custom_call" | custom-call | flops 4000000000 | bytes 8388608 | tf_op jit(solution)/shard_map/pallas_call | solution.py:305
  67.7 0.0 copy-start
  67.8 2.3 %copy.8 = f32[512,512]{1,0:T(8,128)} copy(f32[512,512]{1,0:T(8,128)} %get-tuple-element.4) | data formatting | bytes 2097152
  70.1 0.0 copy-done
  70.1 0.8 %copy.9 = f32[512,256]{1,0:T(8,128)} copy(f32[512,256]{1,0:T(8,128)S(1)} %copy-done) | data formatting | bytes 1048576
Async XLA Ops:
  67.7 2.3 %copy-start = (f32[512,256]{1,0:T(8,128)S(1)}, f32[512,256]{1,0:T(8,128)}, u32[]{:S(2)}) copy-start(f32[512,256]{1,0:T(8,128)} %get-tuple-element.5) | copy-start | bytes 1572868

commit v8 on v7

--- a/solution.py
+++ b/solution.py
@@ -11,8 +11,8 @@
 NY = 2
 N_COL = 2
 NH = 2
-GAP = 5
-SKEW = 4
+GAP = 7
+SKEW = 6
 
 
 def kernel(cfg, a_hbm, l_ref, d_ref, pat, out_ref, diag_ref, a_full, own, ubuf, dbuf, sd, su, fin, yin, acc,

time: 71 us -> 75 us (1.056)
  Pallas kernels: 67.1 us -> 71.1 us
    pallas_call x1, Pallas kernels: 67.1 us -> 71.1 us  [per_device(): pl.pallas_call(functools.partial(kernel, (nz, rt, share, na, s_n, b)), ou...]
where the time goes in v8:
time: 75 us; the launch traced here: 74.9 us
  Pallas kernels  71.1 us (95%)
  local copies, waits for them, and re-layouts  3.12 us (4%)
    pallas_call x1, Pallas kernels, per_device(): pl.pallas_call(functools.partial(kernel, (nz, rt, share, na, s_n, b)), ou...  71.1 us
    unnamed x4, local copies, waits for them, and re-layouts  3.12 us

profile of v8, /device:TPU:0, one launch (start us, length us, event | category | flops | bytes accessed | tf_op | source)
XLA Modules:
  0.0 74.9 jit_solution(9495455062243779631)
XLA Ops:
  0.6 71.1 %shard_map.59 = (f32[512,512]{1,0:T(8,128)}, f32[512,256]{1,0:T(8,128)}) custom-call(bf16[512,2048]{1,0:T(8,128)(2,1)} %a_hbm.1, bf16[512,512]{1,0:T(8,128)(2,1)} %l_ref.1, f32[512,256]{1,0:T(8,128)} %d_ref.1, s32[4,8]{1,0:T(4,128)} %pat.1), custom_call_target="tpu_custom_call" | custom-call | flops 4000000000 | bytes 8388608 | tf_op jit(solution)/shard_map/pallas_call | solution.py:305
  71.7 0.0 copy-start
  71.7 2.3 %copy.8 = f32[512,512]{1,0:T(8,128)} copy(f32[512,512]{1,0:T(8,128)} %get-tuple-element.4) | data formatting | bytes 2097152
  74.1 0.0 copy-done
  74.1 0.8 %copy.9 = f32[512,256]{1,0:T(8,128)} copy(f32[512,256]{1,0:T(8,128)S(1)} %copy-done) | data formatting | bytes 1048576
Async XLA Ops:
  71.7 2.3 %copy-start = (f32[512,256]{1,0:T(8,128)S(1)}, f32[512,256]{1,0:T(8,128)}, u32[]{:S(2)}) copy-start(f32[512,256]{1,0:T(8,128)} %get-tuple-element.5) | copy-start | bytes 1572868
